TPU v7x, 512 devices: a whole 4x4x16 slice. The times are simulated.
512 devices in a mesh: graph: 128 (over z, x, core), dp: 4 (over y).
Axes of the slice: x: 4, y: 4, z: 16, core: 2. Of those that a mesh axis runs over, the one named last changes fastest.
Arguments:
- atoms: bfloat16 [8192, 256], P(('dp', 'graph')), parts along dimension 0, may hold values from -6 to 6
- fetch_rows: int32 [512, 128, 4], P(('dp', 'graph')), parts along dimension 0, may hold values from 0 to 15
- edge_slots: int32 [2, 131072], P(None, ('dp', 'graph')), parts along dimension 1, may hold values from 0 to 511, as said below
- messages: bfloat16 [131072, 1024], P(('dp', 'graph')), parts along dimension 0, may hold values from -6 to 6
- radial: bfloat16 [16, 131072], P(None, ('dp', 'graph')), parts along dimension 1, may hold values from -6 to 6
- angular: bfloat16 [16, 1048576], P(None, ('dp', 'graph')), parts along dimension 1, may hold values from -6 to 6
- trip_edges: int32 [2, 1048576], P(None, ('dp', 'graph')), parts along dimension 1, may hold values from 0 to 255
- trip_blocks: int32 [512], P(('dp', 'graph')), parts along dimension 0, may hold values from 1 to 8, as said below
- reverse_slot: int32 [131072], P(('dp', 'graph')), parts along dimension 0, may hold values from 0 to 255, as said below
- message_weight: bfloat16 [1024, 1024], replicated, may hold values from -0.1875 to 0.1875
- source_weight: bfloat16 [256, 1024], replicated, may hold values from -0.375 to 0.375
- target_weight: bfloat16 [256, 1024], replicated, may hold values from -0.375 to 0.375
- radial_weight: bfloat16 [16, 1024], replicated, may hold values from -1.5 to 1.5
- down_weight: bfloat16 [1024, 128], replicated, may hold values from -0.1875 to 0.1875
- angle_weight: bfloat16 [16, 128], replicated, may hold values from -1.5 to 1.5
- up_ca_weight: bfloat16 [128, 1024], replicated, may hold values from -0.5 to 0.5
- up_ac_weight: bfloat16 [128, 1024], replicated, may hold values from -0.5 to 0.5
Outputs:
- updated: bfloat16 [131072, 1024], P(('dp', 'graph')), parts along dimension 0
- message_grad: bfloat16 [131072, 1024], P(('dp', 'graph')), parts along dimension 0
- atom_grad: float32 [8192, 256], P(('dp', 'graph')), parts along dimension 0
There are 4 independent parts, one for each index of `dp`. A program takes and returns all parts, laid end to end along the dimension named above; an argument that names none is the same for every part. Nothing has to cross between parts.
Inputs may be any that keep to these rules, and one draw needn't show every extreme that they name: `edge_slots`: on each device the 512 slot numbers of its edges use every slot once. `trip_blocks`: triplet slots past the live blocks of a device are padding; some device has all its blocks live. `reverse_slot`: the reverse of an edge on device r lies on device r XOR 1 at the given position, and the reverse of the reverse is the edge itself.
All inputs are finite; a program needn't handle non-finite values.
Results may differ from a plain program's by a relative error of at most 0.0095.
Values may be sent and summed in bfloat16 or wider, within the bound.
A program may use at most 64 MiB of HBM per device.

v0:
```python
import jax
import jax.numpy as jnp
from jax import lax
from jax.sharding import PartitionSpec as P

TBLK = 256


def swapped(block, axis, distance):
    count = lax.axis_size(axis)
    route = []
    for low in range(count):
        high = low | 1 << distance
        if high != low and high < count:
            route += [(low, high), (high, low)]
    return lax.ppermute(block, axis, route)


def silu_grad(values):
    sigma = jax.nn.sigmoid(values)
    return sigma * (1.0 + values * (1.0 - sigma))


def times_trans(left, weight):
    return lax.dot_general(
        left, weight, (((1,), (1,)), ((), ())), preferred_element_type=jnp.float32
    )


def shards(
    atoms,
    fetch_rows,
    edge_slots,
    messages,
    radial,
    angular,
    trip_edges,
    trip_blocks,
    reverse_slot,
    message_weight,
    source_weight,
    target_weight,
    radial_weight,
    down_weight,
    angle_weight,
    up_ca_weight,
    up_ac_weight,
):
    groups = lax.axis_size("graph")
    per_peer = fetch_rows.shape[2]
    local_atoms = atoms.shape[0]
    atom_width = atoms.shape[1]
    edge_count = messages.shape[0]
    wanted = fetch_rows[0]
    asked = lax.all_to_all(wanted, "graph", split_axis=0, concat_axis=0, tiled=True)
    picked = atoms[asked.reshape(-1)].reshape(groups, per_peer, atom_width)
    slot_rows = lax.all_to_all(picked, "graph", split_axis=0, concat_axis=0, tiled=True).reshape(
        groups * per_peer, atom_width
    )
    source_rows = slot_rows[edge_slots[0]]
    target_rows = slot_rows[edge_slots[1]]
    pre = jnp.dot(messages, message_weight, preferred_element_type=jnp.float32)
    pre = pre + jnp.dot(source_rows, source_weight, preferred_element_type=jnp.float32)
    pre = pre + jnp.dot(target_rows, target_weight, preferred_element_type=jnp.float32)
    gate = lax.dot_general(
        radial, radial_weight, (((0,), (0,)), ((), ())), preferred_element_type=jnp.float32
    )
    edge_hidden = (jax.nn.silu(pre) * gate).astype(jnp.bfloat16)
    down = jnp.dot(edge_hidden, down_weight, preferred_element_type=jnp.float32)
    reduced = jax.nn.silu(down).astype(jnp.bfloat16)
    trip_width = down_weight.shape[1]
    live_blocks = trip_blocks[0]

    def block_parts(index):
        start = index * TBLK
        basis_block = lax.dynamic_slice_in_dim(angular, start, TBLK, 1)
        basis = lax.dot_general(
            basis_block, angle_weight, (((0,), (0,)), ((), ())), preferred_element_type=jnp.float32
        )
        targets = lax.dynamic_slice_in_dim(trip_edges[0], start, TBLK, 0)
        sources = lax.dynamic_slice_in_dim(trip_edges[1], start, TBLK, 0)
        return (basis, targets, sources)

    def forward_block(index, total):
        basis, targets, sources = block_parts(index)
        terms = basis * reduced[sources].astype(jnp.float32)
        return total + jax.ops.segment_sum(terms, targets, num_segments=edge_count)

    empty = jnp.zeros((edge_count, trip_width), jnp.float32)
    gathered = lax.fori_loop(0, live_blocks, forward_block, empty).astype(jnp.bfloat16)
    raised_ca = jnp.dot(gathered, up_ca_weight, preferred_element_type=jnp.float32).astype(
        jnp.bfloat16
    )
    raised_ac = jnp.dot(gathered, up_ac_weight, preferred_element_type=jnp.float32).astype(
        jnp.bfloat16
    )
    partner_raised = swapped(raised_ac, "graph", 0)
    raised_back = partner_raised[reverse_slot]
    updated = (raised_ca.astype(jnp.float32) + raised_back.astype(jnp.float32)).astype(jnp.bfloat16)
    lowered = times_trans(updated, up_ca_weight)
    partner_updated = swapped(updated, "graph", 0)
    lowered_back = times_trans(partner_updated[reverse_slot], up_ac_weight)
    lowered_grad = lowered + lowered_back

    def backward_block(index, total):
        basis, targets, sources = block_parts(index)
        terms = basis * lowered_grad[targets]
        return total + jax.ops.segment_sum(terms, sources, num_segments=edge_count)

    reduced_grad = lax.fori_loop(0, live_blocks, backward_block, empty)
    down_grad = (reduced_grad * silu_grad(down)).astype(jnp.bfloat16)
    hidden_grad = times_trans(down_grad, down_weight)
    pre_grad = (hidden_grad * gate * silu_grad(pre)).astype(jnp.bfloat16)
    message_grad = times_trans(pre_grad, message_weight).astype(jnp.bfloat16)
    source_grad = times_trans(pre_grad, source_weight)
    target_grad = times_trans(pre_grad, target_weight)
    both_grads = jnp.concatenate([source_grad, target_grad], axis=0)
    both_slots = jnp.concatenate([edge_slots[0], edge_slots[1]], axis=0)
    slot_grads = jax.ops.segment_sum(both_grads, both_slots, num_segments=groups * per_peer)
    returned = lax.all_to_all(
        slot_grads.reshape(groups, per_peer, atom_width).astype(jnp.bfloat16),
        "graph",
        split_axis=0,
        concat_axis=0,
        tiled=True,
    ).astype(jnp.float32)
    one_hot = (
        asked.reshape(-1)[:, None] == jnp.arange(local_atoms, dtype=jnp.int32)[None, :]
    ).astype(jnp.float32)
    atom_grad = lax.dot_general(
        one_hot,
        returned.reshape(groups * per_peer, atom_width),
        (((0,), (0,)), ((), ())),
        precision=lax.Precision.HIGHEST,
        preferred_element_type=jnp.float32,
    )
    return (updated, message_grad, atom_grad)


def solution(mesh):
    placed = (
        P(("dp", "graph"), None),
        P(("dp", "graph"), None, None),
        P(None, ("dp", "graph")),
        P(("dp", "graph"), None),
        P(None, ("dp", "graph")),
        P(None, ("dp", "graph")),
        P(None, ("dp", "graph")),
        P(("dp", "graph")),
        P(("dp", "graph")),
        P(),
        P(),
        P(),
        P(),
        P(),
        P(),
        P(),
        P(),
    )
    return jax.shard_map(
        shards,
        mesh=mesh,
        in_specs=placed,
        out_specs=(P(("dp", "graph"), None), P(("dp", "graph"), None), P(("dp", "graph"), None)),
        check_vma=False,
    )
```

profile of v0, /device:TPU:1, one launch (start us, length us, event | category | flops | bytes accessed | tf_op | source)
XLA Modules:
  0.0 200.2 jit_solution(7222975405658218403)
XLA Ops:
  0.7 0.9 copy.22
  1.6 35.1 %all_to_all.19 = s32[128,1,4]{2,1,0:T(1,128)S(1)} all-to-all(s32[128,1,4]{2,1,0:T(1,128)S(1)} %bitcast.62), channel_id=1, replica_groups=mesh['graph'=128,'dp'=4] {'graph'}, dimensions={0} | all-to-all | bytes 4096 | tf_op jit(solution)/shard_map/all_to_all | solution.py:55
  36.7 0.5 broadcast.150
  37.2 0.8 reduce.5
  38.0 0.1 reshape.172
  38.2 2.3 %gather_fusion.2 = bf16[512,256]{1,0:T(8,128)(2,1)S(1)} fusion(bf16[16,256]{1,0:T(8,128)(2,1)} %param.21, s32[1024]{0:T(1024)S(1)} %pad_clamp_fusion.5), kind=kCustom, calls=%fused_computation.2 | custom fusion | bytes 526336 | tf_op jit(solution)/shard_map/gather | solution.py:56
  40.5 0.8 reshape.173
  41.2 6.7 %all-to-all-start.1 = ((bf16[128,4,256]{2,1,0:T(4,128)(2,1)}), bf16[128,4,256]{2,1,0:T(4,128)(2,1)}, u32[]{:S(2)}, u32[]{:S(2)}) async-start(bf16[128,4,256]{2,1,0:T(4,128)(2,1)} %reshape.173), calls=%async_computation.1 | async-start | bytes 524288 | tf_op jit(solution)/shard_map/all_to_all | solution.py:57
  48.0 1.3 fusion.24
  49.3 1.7 fusion.23
  51.1 17.1 %all-to-all-done.1 = bf16[128,4,256]{2,1,0:T(4,128)(2,1)} async-done(((bf16[128,4,256]{2,1,0:T(4,128)(2,1)}), bf16[128,4,256]{2,1,0:T(4,128)(2,1)}, u32[]{:S(2)}, u32[]{:S(2)}) %all-to-all-start.1) | async-done | bytes 262176 | tf_op jit(solution)/shard_map/all_to_all | solution.py:57
  68.2 1.0 reshape.174
  69.2 1.2 gather_fusion.3
  70.4 1.8 gather_fusion.4
  72.2 1.5 convolution_add_fusion.1
  73.7 0.3 convolution_add_fusion
  74.1 1.1 multiply_convert_fusion.3
  75.2 5.2 %while.20 = (s32[]{:T(128)}, f32[256,128]{1,0:T(8,128)S(1)}, s32[]{:T(128)}, s32[2,2048]{1,0:T(2,128)S(1)}, bf16[16,2048]{1,0:T(8,128)(2,1)}, /*index=5*/bf16[16...) while((s32[]{:T(128)}, f32[256,128]{1,0:T(8,128)S(1)}, ...), condition=%wide.region_2.3_spmd, body=%wide.region_0.2_spmd.sunk | while | flops 1148678 | bytes 777383 | solution.py:90
  76.0 0.9 gather_fusion
  76.8 0.9 convolution_multiply_fusion.5
  77.8 2.0 scatter_fusion
  80.4 0.3 convolution_convert_fusion.1
  80.7 2.3 %collective-permute-start = (bf16[256,1024]{1,0:T(8,128)(2,1)S(1)}, bf16[256,1024]{1,0:T(8,128)(2,1)S(1)}, u32[]{:S(2)}, u32[]{:S(2)}) collective-permute-start(bf16[256,1024]{1,0:T(8,128)(2,1)S(1)} %convolution_convert_fusion.1), channel_id=1, source_target_pairs={{0,4},{4,0},{8,12},{12,8},{16,20},{20,16},{24,28},{28,24},{32,36},... | collective-permute-start | bytes 1572872 | tf_op jit(solution)/shard_map/ppermute | solution.py:16
  83.1 0.6 pad_clamp_fusion.2
  83.7 1.3 fusion.6
  84.9 1.3 gather_fusion.5
  86.3 2.2 %add_convert_fusion = bf16[256,1024]{1,0:T(8,128)(2,1)} fusion(f32[256,1024]{1,0:T(8,128)} %fusion.6, bf16[256,1024]{1,0:T(8,128)(2,1)S(1)} %gather_fusion.5), kind=kLoop, calls=%fused_computation.32 | loop fusion | flops 786432 | bytes 2097152 | tf_op jit(solution)/shard_map/convert_element_type | solution.py:99
  88.4 2.2 %collective-permute-start.1 = (bf16[256,1024]{1,0:T(8,128)(2,1)}, bf16[256,1024]{1,0:T(8,128)(2,1)S(1)}, u32[]{:S(2)}, u32[]{:S(2)}) collective-permute-start(bf16[256,1024]{1,0:T(8,128)(2,1)} %add_convert_fusion), channel_id=1, source_target_pairs={{0,4},{4,0},{8,12},{12,8},{16,20},{20,16},{24,28},{28,24},{32,36},... | collective-permute-start | bytes 1572872 | tf_op jit(solution)/shard_map/ppermute | solution.py:16
  90.6 0.6 pad_add_fusion
  91.2 1.2 collective-permute-done.1
  92.4 1.3 gather_fusion.6
  93.8 0.3 fusion.25
  94.1 1.4 convolution_add_fusion.2
  95.5 5.1 %while.21 = (s32[]{:T(128)}, f32[256,128]{1,0:T(8,128)S(1)}, s32[]{:T(128)}, s32[2,2048]{1,0:T(2,128)S(1)}, bf16[16,2048]{1,0:T(8,128)(2,1)}, /*index=5*/bf16[16...) while((s32[]{:T(128)}, f32[256,128]{1,0:T(8,128)S(1)}, ...), condition=%wide.region_5.6_spmd, body=%wide.region_3.5_spmd.sunk | while | flops 1115910 | bytes 973991 | solution.py:110
  96.3 0.7 gather_fusion.1
  97.0 0.9 convolution_multiply_fusion.6
  98.0 2.0 scatter_fusion.1
  100.7 2.1 %fusion.5 = bf16[256,1024]{1,0:T(8,128)(2,1)S(1)} fusion(f32[256,1024]{1,0:T(8,128)} %fusion.24, bf16[1024,128]{1,0:T(8,128)(2,1)S(1)} %copy-done.20, f32[256,1024]{1,0:T(8,128)} %copy-done.7, f32[256,128]{1,0:T(8,128)S(1)} %get-tuple-element.80, f32[256,128]{1,0:T(8,128)S(1)} %copy-done.21), kind=kOutput, calls=%fused_computation.26 | convolution fusion | flops 70025216 | bytes 3145728 | tf_op jit(solution)/shard_map/dot_general | solution.py:25
  102.8 0.3 fusion.26
  103.2 1.0 fusion.27
  104.2 3.9 %scatter_custom_fusion.2 = f32[512,256]{1,0:T(8,128)S(1)} fusion(s32[512]{0:T(512)} %pad_add_fusion, f32[256,256]{1,0:T(8,128)} %fusion.27, f32[]{:T(128)} %constant.57, f32[256,256]{1,0:T(8,128)S(1)} %fusion.26, f32[]{:T(128)} %constant.14.clone.1), kind=kCustom, calls=%fused_computation.35 | custom fusion | flops 262144 | bytes 1049600 | tf_op jit(solution)/shard_map/scatter-add | solution.py:119
  108.1 0.8 convert_element_type.56
  108.9 69.9 %all-to-all-start.2 = ((bf16[128,4,256]{2,1,0:T(4,128)(2,1)}), bf16[128,4,256]{2,1,0:T(4,128)(2,1)S(1)}, u32[]{:S(2)}, u32[]{:S(2)}) async-start(bf16[128,4,256]{2,1,0:T(4,128)(2,1)} %convert_element_type.56), calls=%async_computation.2 | async-start | bytes 524288 | tf_op jit(solution)/shard_map/all_to_all | solution.py:120
  178.8 0.1 eq.15
  178.9 1.5 convolution_convert_fusion
  180.4 18.8 %all-to-all-done.2 = bf16[128,4,256]{2,1,0:T(4,128)(2,1)S(1)} async-done(((bf16[128,4,256]{2,1,0:T(4,128)(2,1)}), bf16[128,4,256]{2,1,0:T(4,128)(2,1)S(1)}, u32[]{:S(2)}, u32[]{:S(2)}) %all-to-all-start.2) | async-done | bytes 262176 | tf_op jit(solution)/shard_map/all_to_all | solution.py:120
  199.2 0.1 reshape.175
  199.3 0.9 fusion.13
  (63 shorter events, 0.3 us)
Async XLA Ops:
  0.6 48.7 %copy-start = (bf16[1024,1024]{1,0:T(8,128)(2,1)S(1)}, bf16[1024,1024]{1,0:T(8,128)(2,1)}, u32[]{:S(2)}) copy-start(bf16[1024,1024]{1,0:T(8,128)(2,1)} %param.30) | copy-start | bytes 6291460
  0.6 47.3 %copy-start.16 = (s32[2,256]{1,0:T(2,128)S(1)}, s32[2,256]{1,0:T(2,128)}, u32[]{:S(2)}) copy-start(s32[2,256]{1,0:T(2,128)} %param.23) | copy-start | bytes 6148
  0.7 47.3 %copy-start.15 = (bf16[16,256]{1,0:T(8,128)(2,1)S(1)}, bf16[16,256]{1,0:T(8,128)(2,1)}, u32[]{:S(2)}) copy-start(bf16[16,256]{1,0:T(8,128)(2,1)} %param.25) | copy-start | bytes 24580
  0.7 47.3 %copy-start.14 = (bf16[16,1024]{1,0:T(8,128)(2,1)S(1)}, bf16[16,1024]{1,0:T(8,128)(2,1)}, u32[]{:S(2)}) copy-start(bf16[16,1024]{1,0:T(8,128)(2,1)} %param.33) | copy-start | bytes 98308
  36.7 1.5 copy-start.9
  41.2 27.0 %all-to-all-start.1 = ((bf16[128,4,256]{2,1,0:T(4,128)(2,1)}), bf16[128,4,256]{2,1,0:T(4,128)(2,1)}, u32[]{:S(2)}, u32[]{:S(2)}) async-start(bf16[128,4,256]{2,1,0:T(4,128)(2,1)} %reshape.173), calls=%async_computation.1 | async-start | bytes 524288 | tf_op jit(solution)/shard_map/all_to_all | solution.py:57
  72.2 1.5 copy-start.2
  72.2 1.5 copy-start.11
  72.2 1.8 copy-start.6
  72.2 1.8 copy-start.19
  74.0 1.1 copy-start.7
  74.0 1.1 copy-start.4
  74.0 1.1 copy-start.12
  75.2 5.3 %copy-start.5 = (bf16[128,1024]{1,0:T(8,128)(2,1)S(1)}, bf16[128,1024]{1,0:T(8,128)(2,1)}, u32[]{:S(2)}) copy-start(bf16[128,1024]{1,0:T(8,128)(2,1)} %param.37) | copy-start | bytes 786436
  75.2 7.9 %copy-start.18 = (s32[256]{0:T(256)S(1)}, s32[256]{0:T(256)}, u32[]{:S(2)}) copy-start(s32[256]{0:T(256)} %param.29) | copy-start | bytes 3076
  75.2 8.5 %copy-start.8 = (bf16[128,1024]{1,0:T(8,128)(2,1)S(1)}, bf16[128,1024]{1,0:T(8,128)(2,1)}, u32[]{:S(2)}) copy-start(bf16[128,1024]{1,0:T(8,128)(2,1)} %param.36) | copy-start | bytes 786436
  80.7 4.2 %collective-permute-start = (bf16[256,1024]{1,0:T(8,128)(2,1)S(1)}, bf16[256,1024]{1,0:T(8,128)(2,1)S(1)}, u32[]{:S(2)}, u32[]{:S(2)}) collective-permute-start(bf16[256,1024]{1,0:T(8,128)(2,1)S(1)} %convolution_convert_fusion.1), channel_id=1, source_target_pairs={{0,4},{4,0},{8,12},{12,8},{16,20},{20,16},{24,28},{28,24},{32,36},... | collective-permute-start | bytes 1572872 | tf_op jit(solution)/shard_map/ppermute | solution.py:16
  86.3 4.4 %copy-start.17 = (s32[2,256]{1,0:T(2,128)S(1)}, s32[2,256]{1,0:T(2,128)}, u32[]{:S(2)}) copy-start(s32[2,256]{1,0:T(2,128)} %param.23) | copy-start | bytes 6148
  88.4 4.0 %collective-permute-start.1 = (bf16[256,1024]{1,0:T(8,128)(2,1)}, bf16[256,1024]{1,0:T(8,128)(2,1)S(1)}, u32[]{:S(2)}, u32[]{:S(2)}) collective-permute-start(bf16[256,1024]{1,0:T(8,128)(2,1)} %add_convert_fusion), channel_id=1, source_target_pairs={{0,4},{4,0},{8,12},{12,8},{16,20},{20,16},{24,28},{28,24},{32,36},... | collective-permute-start | bytes 1572872 | tf_op jit(solution)/shard_map/ppermute | solution.py:16
  93.7 1.8 copy-start.13
  95.5 5.1 %copy-start.20 = (bf16[1024,128]{1,0:T(8,128)(2,1)S(1)}, bf16[1024,128]{1,0:T(8,128)(2,1)}, u32[]{:S(2)}) copy-start(bf16[1024,128]{1,0:T(8,128)(2,1)} %param.34) | copy-start | bytes 786436
  95.5 5.1 %copy-start.21 = (f32[256,128]{1,0:T(8,128)S(1)}, f32[256,128]{1,0:T(8,128)}, u32[]{:S(2)}) copy-start(f32[256,128]{1,0:T(8,128)} %get-tuple-element.118) | copy-start | bytes 393220
  100.6 2.2 %copy-start.1 = (bf16[256,1024]{1,0:T(8,128)(2,1)S(1)}, bf16[256,1024]{1,0:T(8,128)(2,1)}, u32[]{:S(2)}) copy-start(bf16[256,1024]{1,0:T(8,128)(2,1)} %param.31) | copy-start | bytes 1572868
  100.7 2.5 %copy-start.3 = (bf16[256,1024]{1,0:T(8,128)(2,1)S(1)}, bf16[256,1024]{1,0:T(8,128)(2,1)}, u32[]{:S(2)}) copy-start(bf16[256,1024]{1,0:T(8,128)(2,1)} %param.32) | copy-start | bytes 1572868
  103.2 75.6 %copy-start.10 = (s32[128,1,4]{2,1,0:T(1,128)S(1)}, s32[128,1,4]{2,1,0:T(1,128)}, u32[]{:S(2)}) copy-start(s32[128,1,4]{2,1,0:T(1,128)} %copy-done.9) | copy-start | bytes 6148
  108.9 90.3 %all-to-all-start.2 = ((bf16[128,4,256]{2,1,0:T(4,128)(2,1)}), bf16[128,4,256]{2,1,0:T(4,128)(2,1)S(1)}, u32[]{:S(2)}, u32[]{:S(2)}) async-start(bf16[128,4,256]{2,1,0:T(4,128)(2,1)} %convert_element_type.56), calls=%async_computation.2 | async-start | bytes 524288 | tf_op jit(solution)/shard_map/all_to_all | solution.py:120
where the time goes:
time: 203 us; the launch traced here: 200 us
  starting transfers between devices  81.1 us (40%)
  waiting for transfers between devices  37.2 us (18%)
  blocking collectives  35.1 us (17%)
  matrix products  16.9 us (8%)
  local copies, waits for them, and re-layouts  13.9 us (7%)
  other arithmetic  12.1 us (6%)
  loops' own time  2.83 us (1%)
    all_to_all x1, starting transfers between devices, shards(): lax.all_to_all(slot_grads.reshape(groups, per_peer, atom_width).astype(jn...  69.9 us
    all_to_all x1, blocking collectives, shards(): lax.all_to_all(wanted, 'graph', split_axis=0, concat_axis=0, tiled=True)  35.1 us
    all_to_all x1, waiting for transfers between devices, shards(): lax.all_to_all(slot_grads.reshape(groups, per_peer, atom_width).astype(jn...  18.8 us
    all_to_all x1, waiting for transfers between devices, shards(): lax.all_to_all(picked, 'graph', split_axis=0, concat_axis=0, tiled=True)  17.1 us
    dot_general x6, matrix products, times_trans(): lax.dot_general(left, weight, (((1,), (1,)), ((), ())), preferred_element...  6.76 us
    all_to_all x1, starting transfers between devices, shards(): lax.all_to_all(picked, 'graph', split_axis=0, concat_axis=0, tiled=True)  6.71 us
    ppermute x2, starting transfers between devices, swapped(): return lax.ppermute(block, axis, route)  4.49 us
  transfers between devices with their start and end apart: 4, of which 3 were waited for; matrix products, arithmetic and copies ran while one was open for 4% of the time, Pallas kernels for 0%

commit v1 on v0

v1 whole, which is shorter than its diff:
```python
import functools

import jax
import jax.numpy as jnp
from jax import lax
from jax.experimental import pallas as pl
from jax.experimental.pallas import tpu as pltpu
from jax.sharding import PartitionSpec as P

TBLK = 256
PLANE = 8
VMEM = 62 * 1024 * 1024
F32 = jnp.float32
BF16 = jnp.bfloat16
MESH = pl.DeviceIdType.MESH


def iota(shape, dim):
    return lax.broadcasted_iota(jnp.int32, shape, dim)


def dot(left, right):
    return jnp.dot(left, right, preferred_element_type=F32)


def dot_nt(left, right):
    return lax.dot_general(left, right, (((1,), (1,)), ((), ())), preferred_element_type=F32)


def hot(mask):
    return jnp.where(mask, 1.0, 0.0).astype(BF16)


def column(row):
    count = row.shape[1]
    tall = jnp.broadcast_to(row.astype(F32), (128, count))
    return jnp.transpose(tall)


def hot_rows(row, width):
    wide = column(row).astype(jnp.int32)
    parts = [hot(wide == iota(wide.shape, 1) + start) for start in range(0, width, 128)]
    return jnp.concatenate(parts, axis=1)


def kernel(
    plane,
    count,
    blocks_ref,
    *refs,
):
    n_in = 16
    hbm = refs[:n_in]
    updated_out, message_out, atom_out = refs[n_in : n_in + 3]
    vm = refs[n_in + 3 : 2 * n_in + 3]
    (
        atoms,
        fetch,
        slots_in,
        trips,
        reverse,
        angular,
        angle_w,
        radial,
        radial_w,
        down_w,
        up_ca,
        messages,
        message_w,
        source_w,
        up_ac,
        target_w,
    ) = vm
    (
        st,
        tt,
        bt,
        gate,
        pre,
        hidden,
        grad,
        down_t,
        mix,
        edge_rows,
        slot_cols,
        rev_cols,
        sel,
        sel_t,
        pair,
        table,
        want_out,
        want_in,
        rows_out,
        rows_in,
        gather_in,
        back_out,
        back_in,
        part_out,
        part_in,
        updated_v,
        message_v,
        atom_v,
        in_sem,
        out_sem,
        atom_send,
        atom_recv,
        want_send,
        want_recv,
        rows_send,
        rows_recv,
        pair_send,
        pair_recv,
        back_send,
        back_recv,
        part_send,
        part_recv,
    ) = refs[2 * n_in + 3 :]
    depth = count // plane
    per_peer = fetch.shape[0]
    local = atoms.shape[0]
    column_atoms = depth * local
    share = depth * per_peer
    edges, width = messages.shape
    trip_count = trips.shape[1]
    tri = down_w.shape[1]

    me = lax.axis_index("graph")
    my_z, my_q = me // plane, me % plane

    def z_peer(step):
        return (my_z + step) % depth

    def q_peer(step):
        return (my_q + step) % plane

    def at(z, q):
        return {"graph": z * plane + q}

    def remote(src, dst, send, recv, where):
        return pltpu.make_async_remote_copy(
            src_ref=src, dst_ref=dst, send_sem=send, recv_sem=recv, device_id=where, device_id_type=MESH
        )

    barrier = pltpu.get_barrier_semaphore()

    @pl.loop(1, depth)
    def _(step):
        pl.semaphore_signal(barrier, inc=1, device_id=at(z_peer(step), my_q), device_id_type=MESH)

    @pl.loop(1, plane)
    def _(step):
        pl.semaphore_signal(barrier, inc=1, device_id=at(my_z, q_peer(step)), device_id_type=MESH)

    loads = [pltpu.make_async_copy(hbm[i], vm[i], in_sem.at[i]) for i in range(n_in)]
    for load in loads:
        load.start()

    pl.semaphore_wait(barrier, depth + plane - 2)

    def atom_copy(step, slot):
        return remote(atoms, table.at[slot], atom_send.at[step], atom_recv.at[slot], at(z_peer(step), my_q))

    loads[0].wait()

    @pl.loop(1, depth)
    def _(step):
        atom_copy(step, my_z).start()

    table[my_z] = atoms[...]

    loads[1].wait()
    flat = jnp.concatenate([fetch[c : c + 1, :] for c in range(per_peer)], axis=1)
    flat = jnp.broadcast_to(flat.astype(F32), (8, per_peer * count)).astype(BF16)
    from_peer = iota((per_peer * count, 128), 0)
    to_lane = iota((per_peer * count, 128), 1)
    lane = iota((8, 128), 1)
    for q in range(plane):
        pick = hot(
            (from_peer // count == to_lane // depth)
            & (from_peer % count == (to_lane % depth) * plane + q)
        )
        ids = dot(flat, pick).astype(jnp.int32) + (lane % depth) * local
        want_out[q] = jnp.where(lane < share, ids, -1)[0:1, :]

    def want_copy(step, slot):
        return remote(
            want_out.at[q_peer(step)], want_in.at[slot], want_send.at[step], want_recv.at[slot], at(my_z, q_peer(step))
        )

    @pl.loop(1, plane)
    def _(step):
        want_copy(step, my_q).start()

    want_in[my_q] = want_out[my_q]

    loads[3].wait()
    live = blocks_ref[0] * TBLK
    chunk = 512

    @pl.loop(0, trip_count // chunk)
    def _(i):
        span = pl.ds(pl.multiple_of(i * chunk, chunk), chunk)
        edge = iota((edges, chunk), 0)
        at_trip = iota((1, chunk), 1) + i * chunk
        targets = jnp.where(at_trip < live, trips[0:1, span], -1)
        tt[:, span] = hot(edge == targets)
        st[:, span] = hot(edge == trips[1:2, span])

    loads[5].wait()
    loads[6].wait()
    bt[...] = dot(jnp.transpose(angle_w[...].astype(F32)).astype(BF16), angular[...])

    loads[2].wait()
    loads[4].wait()
    slot = slots_in[...]
    owner = slot // per_peer
    slot = (owner % plane) * share + (slot % per_peer) * depth + owner // plane
    total = plane * share
    for role in range(2):
        row = slot[role : role + 1, :]
        edge_rows[role] = hot_rows(row, total)
        slot_cols[:, role * edges : (role + 1) * edges] = hot(iota((total, edges), 0) == row)
    rev_cols[...] = hot(iota((edges, edges), 0) == reverse[...])

    def want_wait(step):
        want_copy(step, q_peer(step)).wait_recv()

    @pl.loop(1, plane)
    def _(step):
        want_wait(step)

    for q in range(plane):
        sel[q * share : (q + 1) * share, :] = hot_rows(want_in[q], column_atoms)[:share]

    loads[9].wait()
    down_t[...] = jnp.transpose(down_w[...].astype(F32)).astype(BF16)

    @pl.loop(1, depth)
    def _(step):
        atom_copy(step, z_peer(step)).wait_recv()

    rows = dot(sel[...], table[...].reshape(column_atoms, atoms.shape[1])).astype(BF16)
    rows_out[...] = rows.reshape(rows_out.shape)

    def rows_copy(step, slot_at):
        return remote(
            rows_out.at[q_peer(step)], rows_in.at[slot_at], rows_send.at[step], rows_recv.at[slot_at], at(my_z, q_peer(step))
        )

    @pl.loop(1, plane)
    def _(step):
        rows_copy(step, my_q).start()

    rows_in[my_q] = rows_out[my_q]

    sel_t[...] = jnp.transpose(sel[...].astype(F32)).astype(BF16)
    loads[7].wait()
    loads[8].wait()
    gate[...] = dot(jnp.transpose(radial[...].astype(F32)).astype(BF16), radial_w[...])
    loads[10].wait()
    loads[14].wait()
    same = dot_nt(up_ca[...], up_ca[...]) + dot_nt(up_ac[...], up_ac[...])
    cross = dot_nt(up_ac[...], up_ca[...])
    cross = cross + jnp.transpose(cross)
    both = jnp.concatenate([same, cross], axis=1)
    high = both.astype(BF16)
    mix[:tri, :] = high
    mix[tri:, :] = (both - high.astype(F32)).astype(BF16)
    loads[11].wait()
    loads[12].wait()
    tile = 256

    @pl.loop(0, width // tile)
    def _(i):
        span = pl.ds(pl.multiple_of(i * tile, tile), tile)
        pre[:, span] = dot(messages[...], message_w[:, span])

    loads[13].wait()
    loads[15].wait()

    @pl.loop(1, plane)
    def _(step):
        rows_copy(step, q_peer(step)).wait_recv()

    slot_rows = rows_in[...].reshape(total, atoms.shape[1])
    source_rows = dot(edge_rows[0], slot_rows).astype(BF16)
    target_rows = dot(edge_rows[1], slot_rows).astype(BF16)
    down = jnp.zeros((tri, edges), F32)
    for start in range(0, width, tile):
        span = slice(start, start + tile)
        part = pre[:, span] + dot(source_rows, source_w[:, span]) + dot(target_rows, target_w[:, span])
        pre[:, span] = part
        hidden[:, span] = (part * jax.nn.sigmoid(part) * gate[:, span]).astype(BF16)
        down = down + dot_nt(down_t[:, span], hidden[:, span])
    reduced = (down * jax.nn.sigmoid(down)).astype(BF16)
    terms = (dot(reduced, st[...]) * bt[...]).astype(BF16)
    gathered = dot_nt(terms, tt[...]).astype(BF16)
    pair[:tri, :] = gathered

    pair_copy = remote(
        pair.at[pl.ds(0, tri)], gather_in, pair_send, pair_recv, at(my_z, my_q + 1 - 2 * (my_q % 2))
    )
    pair_copy.start()

    sigma = jax.nn.sigmoid(down)
    down_slope = sigma * (1.0 + down * (1.0 - sigma))
    for start in range(0, width, tile):
        span = slice(start, start + tile)
        part = pre[:, span]
        sigma = jax.nn.sigmoid(part)
        gate[:, span] = gate[:, span] * (sigma * (1.0 + part * (1.0 - sigma)))

    pair_copy.wait_recv()
    pair[tri:, :] = dot(gather_in[...], rev_cols[...]).astype(BF16)
    lowered = dot(mix[...], pair[...])
    lowered = (lowered[:tri] + lowered[tri:]).astype(BF16)

    terms = (dot(lowered, tt[...]) * bt[...]).astype(BF16)
    down_grad = dot_nt(terms, st[...]) * down_slope
    down_grad = jnp.transpose(down_grad).astype(BF16)
    ends = [jnp.zeros((edges, atoms.shape[1]), F32) for _ in range(2)]
    for start in range(0, width, tile):
        span = slice(start, start + tile)
        part = (dot(down_grad, down_t[:, span]) * gate[:, span]).astype(BF16)
        grad[:, span] = part
        ends[0] = ends[0] + dot_nt(part, source_w[:, span])
        ends[1] = ends[1] + dot_nt(part, target_w[:, span])
    ends = jnp.concatenate([ends[0].astype(BF16), ends[1].astype(BF16)], axis=0)
    back_out[...] = dot(slot_cols[...], ends).astype(BF16).reshape(back_out.shape)

    def back_copy(step, slot_at):
        return remote(
            back_out.at[q_peer(step)], back_in.at[slot_at], back_send.at[step], back_recv.at[slot_at], at(my_z, q_peer(step))
        )

    @pl.loop(1, plane)
    def _(step):
        back_copy(step, my_q).start()

    back_in[my_q] = back_out[my_q]

    mixed = jnp.transpose(pair[...].astype(F32)).astype(BF16)
    for start in range(0, width, tile):
        span = slice(start, start + tile)
        raised = dot(mixed[:, :tri], up_ca[:, span]) + dot(mixed[:, tri:], up_ac[:, span])
        updated_v[:, span] = raised.astype(BF16)
    updated_copy = pltpu.make_async_copy(updated_v, updated_out, out_sem.at[0])
    updated_copy.start()

    @pl.loop(1, plane)
    def _(step):
        back_copy(step, q_peer(step)).wait_recv()

    part = dot(sel_t[...], back_in[...].reshape(total, atoms.shape[1]))
    part_out[...] = part.astype(BF16).reshape(part_out.shape)

    def part_copy(step, slot_at):
        return remote(
            part_out.at[z_peer(step)], part_in.at[slot_at], part_send.at[step], part_recv.at[slot_at], at(z_peer(step), my_q)
        )

    @pl.loop(1, depth)
    def _(step):
        part_copy(step, my_z).start()

    part_in[my_z] = part_out[my_z]

    @pl.loop(0, width // tile)
    def _(i):
        span = pl.ds(pl.multiple_of(i * tile, tile), tile)
        message_v[:, span] = dot_nt(grad[...], message_w[span, :]).astype(BF16)

    message_copy = pltpu.make_async_copy(message_v, message_out, out_sem.at[1])
    message_copy.start()

    @pl.loop(1, depth)
    def _(step):
        part_copy(step, z_peer(step)).wait_recv()

    owned = part_in[0].astype(F32)
    for z in range(1, depth):
        owned = owned + part_in[z].astype(F32)
    atom_v[...] = owned
    atom_copy_out = pltpu.make_async_copy(atom_v, atom_out, out_sem.at[2])
    atom_copy_out.start()

    @pl.loop(1, depth)
    def _(step):
        atom_copy(step, my_z).wait_send()
        part_copy(step, my_z).wait_send()

    @pl.loop(1, plane)
    def _(step):
        want_copy(step, my_q).wait_send()
        rows_copy(step, my_q).wait_send()
        back_copy(step, my_q).wait_send()

    pair_copy.wait_send()
    updated_copy.wait()
    message_copy.wait()
    atom_copy_out.wait()


def shards(
    atoms,
    fetch_rows,
    edge_slots,
    messages,
    radial,
    angular,
    trip_edges,
    trip_blocks,
    reverse_slot,
    message_weight,
    source_weight,
    target_weight,
    radial_weight,
    down_weight,
    angle_weight,
    up_ca_weight,
    up_ac_weight,
):
    count = lax.axis_size("graph")
    plane = PLANE
    depth = count // plane
    local, atom_width = atoms.shape
    edges, width = messages.shape
    tri = down_weight.shape[1]
    trip_count = trip_edges.shape[1]
    per_peer = fetch_rows.shape[2]
    share = depth * per_peer
    total = plane * share
    fetch = jnp.transpose(fetch_rows[0])
    operands = (
        atoms,
        fetch,
        edge_slots,
        trip_edges,
        reverse_slot.reshape(1, edges),
        angular,
        angle_weight,
        radial,
        radial_weight,
        down_weight,
        up_ca_weight,
        messages,
        message_weight,
        source_weight,
        up_ac_weight,
        target_weight,
    )
    V = pltpu.VMEM
    DMA = pltpu.SemaphoreType.DMA
    scratch = [V(x.shape, x.dtype) for x in operands] + [
        V((edges, trip_count), BF16),
        V((edges, trip_count), BF16),
        V((tri, trip_count), F32),
        V((edges, width), F32),
        V((edges, width), F32),
        V((edges, width), BF16),
        V((edges, width), BF16),
        V((tri, width), BF16),
        V((2 * tri, 2 * tri), BF16),
        V((2, edges, total), BF16),
        V((total, 2 * edges), BF16),
        V((edges, edges), BF16),
        V((total, depth * local), BF16),
        V((depth * local, total), BF16),
        V((2 * tri, edges), BF16),
        V((depth, local, atom_width), BF16),
        V((plane, 1, 128), jnp.int32),
        V((plane, 1, 128), jnp.int32),
        V((plane, share, atom_width), BF16),
        V((plane, share, atom_width), BF16),
        V((tri, edges), BF16),
        V((plane, share, atom_width), BF16),
        V((plane, share, atom_width), BF16),
        V((depth, local, atom_width), BF16),
        V((depth, local, atom_width), BF16),
        V((edges, width), BF16),
        V((edges, width), BF16),
        V((local, atom_width), F32),
        DMA((16,)),
        DMA((3,)),
        DMA((depth,)),
        DMA((depth,)),
        DMA((plane,)),
        DMA((plane,)),
        DMA((plane,)),
        DMA((plane,)),
        DMA,
        DMA,
        DMA((plane,)),
        DMA((plane,)),
        DMA((depth,)),
        DMA((depth,)),
    ]
    return pl.pallas_call(
        functools.partial(kernel, plane, count),
        out_shape=(
            jax.ShapeDtypeStruct((edges, width), BF16),
            jax.ShapeDtypeStruct((edges, width), BF16),
            jax.ShapeDtypeStruct((local, atom_width), F32),
        ),
        in_specs=[pl.BlockSpec(memory_space=pltpu.SMEM)] + [pl.BlockSpec(memory_space=pl.ANY)] * len(operands),
        out_specs=[pl.BlockSpec(memory_space=pl.ANY)] * 3,
        scratch_shapes=scratch,
        compiler_params=pltpu.CompilerParams(
            collective_id=0, has_side_effects=True, vmem_limit_bytes=VMEM
        ),
        cost_estimate=pl.CostEstimate(flops=3_000_000_000, bytes_accessed=8_000_000, transcendentals=1_000_000),
    )(trip_blocks, *operands)


def solution(mesh):
    both = ("dp", "graph")
    rows, lanes = P(both, None), P(None, both)
    placed = (
        rows,
        P(both, None, None),
        lanes,
        rows,
        lanes,
        lanes,
        lanes,
        P(both),
        P(both),
    ) + (P(),) * 8
    return jax.shard_map(
        shards,
        mesh=mesh,
        in_specs=placed,
        out_specs=(rows, rows, rows),
        check_vma=False,
    )
```

time: 203 us -> 60 us (0.30); the launches traced: 200 us -> 59.9 us
  starting transfers between devices: 81.1 us -> 0 us
  Pallas kernels: 0 us -> 54.2 us
  waiting for transfers between devices: 37.2 us -> 0 us
  blocking collectives: 35.1 us -> 0 us
  matrix products: 16.9 us -> 0 us
  other arithmetic: 12.1 us -> 0 us
  local copies, waits for them, and re-layouts: 13.9 us -> 4.35 us
  loops' own time: 2.83 us -> 0 us
    all_to_all x2 -> x0, starting transfers between devices: 76.6 us -> none  [the longest x1 69.9 us: shards(): lax.all_to_all(slot_grads.reshape(groups, per_peer, atom_width).astype(jn...]
    pallas_call x0 -> x1, Pallas kernels: none -> 54.2 us  [shards(): pl.pallas_call(functools.partial(kernel, plane, count), out_shape=(jax.Sh...]
    all_to_all x2 -> x0, waiting for transfers between devices: 35.9 us -> none  [the longest x1 18.8 us: shards(): lax.all_to_all(slot_grads.reshape(groups, per_peer, atom_width).astype(jn...]
    all_to_all x1 -> x0, blocking collectives: 35.1 us -> none  [shards(): lax.all_to_all(wanted, 'graph', split_axis=0, concat_axis=0, tiled=True)]
    dot_general x16 -> x0, matrix products: 16.9 us -> none  [the longest x6 6.76 us: times_trans(): lax.dot_general(left, weight, (((1,), (1,)), ((), ())), preferred_element...]
    gather x7 -> x0, local copies, waits for them, and re-layouts: 9.41 us -> none  [the longest x1 2.26 us: shards(): picked = atoms[asked.reshape(-1)].reshape(groups, per_peer, atom_width)]
    scatter-add x3 -> x0, other arithmetic: 7.87 us -> none  [the longest x1 3.86 us: shards(): jax.ops.segment_sum(both_grads, both_slots, num_segments=groups * per_peer)]
    ppermute x2 -> x0, starting transfers between devices: 4.49 us -> none  [swapped(): return lax.ppermute(block, axis, route)]
  transfers between devices with their start and end apart: 4 -> 0, of which waited for: 3 -> 0; matrix products, arithmetic and copies ran while one was open for 4% -> 0% of each run, Pallas kernels for 0% -> 0%
where the time goes in v1:
time: 60 us; the launch traced here: 59.9 us
  Pallas kernels  54.2 us (90%)
  local copies, waits for them, and re-layouts  4.35 us (7%)
  between operations  1.3 us (2%)
    pallas_call x1, Pallas kernels, shards(): pl.pallas_call(functools.partial(kernel, plane, count), out_shape=(jax.Sh...  54.2 us
    unnamed x5, local copies, waits for them, and re-layouts  4.35 us

profile of v1, /device:TPU:1, one launch (start us, length us, event | category | flops | bytes accessed | tf_op | source)
XLA Modules:
  0.0 59.9 jit_solution(10307812795830382177)
XLA Ops:
  1.3 54.2 %shard_map.184 = (bf16[256,1024]{1,0:T(8,128)(2,1)}, bf16[256,1024]{1,0:T(8,128)(2,1)}, f32[16,256]{1,0:T(8,128)}) custom-call(s32[1]{0:T(128)S(6)} %copy.23.blocks_ref, bf16[16,256]{1,0:T(8,128)(2,1)} %refs_0_.1, s32[4,128]{1,0:T(4,128)} %bitcast.4, s32[2,256]{1,0:T(2,128)} %refs_2_.1, s32[2,2048]{1,0:T(2,128)} %refs_3_.1, s32[1,256]{1,0:T(1,128)} %bitcast.5, ...), custom_call_target="tpu_custom_call" | custom-call | flops 3000000000 | bytes 8000000 | tf_op jit(solution)/shard_map/pallas_call | solution.py:498
  55.5 0.0 copy-start
  55.5 1.9 %copy.24 = bf16[256,1024]{1,0:T(8,128)(2,1)} copy(bf16[256,1024]{1,0:T(8,128)(2,1)} %get-tuple-element.6) | data formatting | bytes 1048576
  57.4 1.9 %copy.25 = bf16[256,1024]{1,0:T(8,128)(2,1)} copy(bf16[256,1024]{1,0:T(8,128)(2,1)} %get-tuple-element.7) | data formatting | bytes 1048576
  59.2 0.0 copy-done
  59.2 0.6 %copy.26 = f32[16,256]{1,0:T(8,128)} copy(f32[16,256]{1,0:T(8,128)S(1)} %copy-done) | data formatting | bytes 32768
Async XLA Ops:
  55.5 3.8 %copy-start = (f32[16,256]{1,0:T(8,128)S(1)}, f32[16,256]{1,0:T(8,128)}, u32[]{:S(2)}) copy-start(f32[16,256]{1,0:T(8,128)} %get-tuple-element.8) | copy-start | bytes 49156

commit v2 on v1

--- a/solution.py
+++ b/solution.py
@@ -9,7 +9,7 @@
 
 TBLK = 256
 PLANE = 8
-VMEM = 62 * 1024 * 1024
+VMEM = 56 * 1024 * 1024
 F32 = jnp.float32
 BF16 = jnp.bfloat16
 MESH = pl.DeviceIdType.MESH
@@ -46,13 +46,12 @@
 def kernel(
     plane,
     count,
-    blocks_ref,
     *refs,
 ):
     n_in = 16
-    hbm = refs[:n_in]
-    updated_out, message_out, atom_out = refs[n_in : n_in + 3]
-    vm = refs[n_in + 3 : 2 * n_in + 3]
+    blocks_hbm, *hbm = refs[: n_in + 1]
+    updated_out, message_out, atom_out = refs[n_in + 1 : n_in + 4]
+    vm = refs[n_in + 4 : 2 * n_in + 4]
     (
         atoms,
         fetch,
@@ -97,11 +96,8 @@
         back_in,
         part_out,
         part_in,
-        updated_v,
-        message_v,
-        atom_v,
+        blocks,
         in_sem,
-        out_sem,
         atom_send,
         atom_recv,
         want_send,
@@ -114,7 +110,7 @@
         back_recv,
         part_send,
         part_recv,
-    ) = refs[2 * n_in + 3 :]
+    ) = refs[2 * n_in + 4 :]
     depth = count // plane
     per_peer = fetch.shape[0]
     local = atoms.shape[0]
@@ -127,11 +123,14 @@
     me = lax.axis_index("graph")
     my_z, my_q = me // plane, me % plane
 
+    def far_first(step, size):
+        return size // 2 + (step // 2) * (2 * (step % 2) - 1)
+
     def z_peer(step):
-        return (my_z + step) % depth
+        return (my_z + far_first(step, depth)) % depth
 
     def q_peer(step):
-        return (my_q + step) % plane
+        return (my_q + far_first(step, plane)) % plane
 
     def at(z, q):
         return {"graph": z * plane + q}
@@ -152,6 +151,7 @@
         pl.semaphore_signal(barrier, inc=1, device_id=at(my_z, q_peer(step)), device_id_type=MESH)
 
     loads = [pltpu.make_async_copy(hbm[i], vm[i], in_sem.at[i]) for i in range(n_in)]
+    loads.append(pltpu.make_async_copy(blocks_hbm, blocks, in_sem.at[n_in]))
     for load in loads:
         load.start()
 
@@ -194,7 +194,8 @@
     want_in[my_q] = want_out[my_q]
 
     loads[3].wait()
-    live = blocks_ref[0] * TBLK
+    loads[n_in].wait()
+    live = blocks[...] * TBLK
     chunk = 512
 
     @pl.loop(0, trip_count // chunk)
@@ -343,9 +344,7 @@
     for start in range(0, width, tile):
         span = slice(start, start + tile)
         raised = dot(mixed[:, :tri], up_ca[:, span]) + dot(mixed[:, tri:], up_ac[:, span])
-        updated_v[:, span] = raised.astype(BF16)
-    updated_copy = pltpu.make_async_copy(updated_v, updated_out, out_sem.at[0])
-    updated_copy.start()
+        updated_out[:, span] = raised.astype(BF16)
 
     @pl.loop(1, plane)
     def _(step):
@@ -368,10 +367,8 @@
     @pl.loop(0, width // tile)
     def _(i):
         span = pl.ds(pl.multiple_of(i * tile, tile), tile)
-        message_v[:, span] = dot_nt(grad[...], message_w[span, :]).astype(BF16)
-
-    message_copy = pltpu.make_async_copy(message_v, message_out, out_sem.at[1])
-    message_copy.start()
+        message_out[:, span] = dot_nt(grad[...], message_w[span, :]).astype(BF16)
+
 
     @pl.loop(1, depth)
     def _(step):
@@ -380,9 +377,7 @@
     owned = part_in[0].astype(F32)
     for z in range(1, depth):
         owned = owned + part_in[z].astype(F32)
-    atom_v[...] = owned
-    atom_copy_out = pltpu.make_async_copy(atom_v, atom_out, out_sem.at[2])
-    atom_copy_out.start()
+    atom_out[...] = owned
 
     @pl.loop(1, depth)
     def _(step):
@@ -396,9 +391,6 @@
         back_copy(step, my_q).wait_send()
 
     pair_copy.wait_send()
-    updated_copy.wait()
-    message_copy.wait()
-    atom_copy_out.wait()
 
 
 def shards(
@@ -477,11 +469,8 @@
         V((plane, share, atom_width), BF16),
         V((depth, local, atom_width), BF16),
         V((depth, local, atom_width), BF16),
-        V((edges, width), BF16),
-        V((edges, width), BF16),
-        V((local, atom_width), F32),
-        DMA((16,)),
-        DMA((3,)),
+        V((1, 1), jnp.int32),
+        DMA((17,)),
         DMA((depth,)),
         DMA((depth,)),
         DMA((plane,)),
@@ -498,18 +487,18 @@
     return pl.pallas_call(
         functools.partial(kernel, plane, count),
         out_shape=(
-            jax.ShapeDtypeStruct((edges, width), BF16),
-            jax.ShapeDtypeStruct((edges, width), BF16),
-            jax.ShapeDtypeStruct((local, atom_width), F32),
+            pltpu.VMEM((edges, width), BF16),
+            pltpu.VMEM((edges, width), BF16),
+            pltpu.VMEM((local, atom_width), F32),
         ),
-        in_specs=[pl.BlockSpec(memory_space=pltpu.SMEM)] + [pl.BlockSpec(memory_space=pl.ANY)] * len(operands),
-        out_specs=[pl.BlockSpec(memory_space=pl.ANY)] * 3,
+        in_specs=[pl.BlockSpec(memory_space=pl.ANY)] * (1 + len(operands)),
+        out_specs=[pl.BlockSpec(memory_space=pltpu.VMEM)] * 3,
         scratch_shapes=scratch,
         compiler_params=pltpu.CompilerParams(
             collective_id=0, has_side_effects=True, vmem_limit_bytes=VMEM
         ),
         cost_estimate=pl.CostEstimate(flops=3_000_000_000, bytes_accessed=8_000_000, transcendentals=1_000_000),
-    )(trip_blocks, *operands)
+    )(trip_blocks.reshape(1, 1), *operands)
 
 
 def solution(mesh):

time: 60 us -> 53.2 us (0.89)
  the two profiles are of different devices: /device:TPU:1 before, /device:TPU:24 now
where the time goes in v2:
time: 53.2 us; the launch traced here: 53.1 us
  Pallas kernels  49.6 us (93%)
  local copies, waits for them, and re-layouts  2.19 us (4%)
  between operations  1.29 us (2%)
    pallas_call x1, Pallas kernels, shards(): pl.pallas_call(functools.partial(kernel, plane, count), out_shape=(pltpu....  49.6 us
    unnamed x3, local copies, waits for them, and re-layouts  2.19 us

profile of v2, /device:TPU:24, one launch (start us, length us, event | category | flops | bytes accessed | tf_op | source)
XLA Modules:
  0.0 53.1 jit_solution(1271441210968209515)
XLA Ops:
  1.3 49.6 %shard_map.184 = (bf16[256,1024]{1,0:T(8,128)(2,1)S(1)}, bf16[256,1024]{1,0:T(8,128)(2,1)S(1)}, f32[16,256]{1,0:T(8,128)S(1)}) custom-call(s32[1,1]{1,0:T(1,128)} %bitcast.5.refs_0_, bf16[16,256]{1,0:T(8,128)(2,1)} %refs_1_.1, s32[4,128]{1,0:T(4,128)} %bitcast.6, s32[2,256]{1,0:T(2,128)} %refs_3_.1, s32[2,2048]{1,0:T(2,128)} %refs_4_.1, s32[1,256]{1,0:T(1,128)} %bitcast.7, ...), custom_call_target="tpu_custom_call" | custom-call | flops 3000000000 | bytes 8000000 | tf_op jit(solution)/shard_map/pallas_call | solution.py:487
  50.9 0.8 %copy.23 = bf16[256,1024]{1,0:T(8,128)(2,1)} copy(bf16[256,1024]{1,0:T(8,128)(2,1)S(1)} %get-tuple-element.3) | data formatting | bytes 1048576
  51.7 0.6 %copy.25 = f32[16,256]{1,0:T(8,128)} copy(f32[16,256]{1,0:T(8,128)S(1)} %get-tuple-element.5) | data formatting | bytes 32768
  52.3 0.8 %copy.24 = bf16[256,1024]{1,0:T(8,128)(2,1)} copy(bf16[256,1024]{1,0:T(8,128)(2,1)S(1)} %get-tuple-element.4) | data formatting | bytes 1048576

commit v3 on v2

v3 whole, which is shorter than its diff:
```python
import functools

import jax
import jax.numpy as jnp
from jax import lax
from jax.experimental import pallas as pl
from jax.experimental.pallas import tpu as pltpu
from jax.sharding import PartitionSpec as P

TBLK = 256
PLANE = 8
VMEM = 56 * 1024 * 1024
F32 = jnp.float32
BF16 = jnp.bfloat16
MESH = pl.DeviceIdType.MESH


def iota(shape, dim):
    return lax.broadcasted_iota(jnp.int32, shape, dim)


def dot(left, right):
    return jnp.dot(left, right, preferred_element_type=F32)


def dot_nt(left, right):
    return lax.dot_general(left, right, (((1,), (1,)), ((), ())), preferred_element_type=F32)


def hot(mask):
    return jnp.where(mask, 1.0, 0.0).astype(BF16)


def column(row):
    count = row.shape[1]
    tall = jnp.broadcast_to(row.astype(F32), (128, count))
    return jnp.transpose(tall)


def hot_rows(row, width):
    wide = column(row).astype(jnp.int32)
    parts = [hot(wide == iota(wide.shape, 1) + start) for start in range(0, width, 128)]
    return jnp.concatenate(parts, axis=1)


def kernel(
    plane,
    count,
    *refs,
):
    n_in = 16
    blocks_hbm, *hbm = refs[: n_in + 1]
    updated_out, message_out, atom_out = refs[n_in + 1 : n_in + 4]
    vm = refs[n_in + 4 : 2 * n_in + 4]
    (
        atoms,
        fetch,
        slots_in,
        trips,
        reverse,
        angular,
        angle_w,
        radial,
        radial_w,
        down_w,
        up_ca,
        messages,
        message_w,
        source_w,
        up_ac,
        target_w,
    ) = vm
    (
        st,
        tt,
        bt,
        gate,
        pre,
        hidden,
        grad,
        down_t,
        rt,
        y,
        mix,
        edge_rows,
        slot_cols,
        rev_cols,
        sel,
        sel_t,
        gather_out,
        table,
        want_out,
        want_in,
        rows_out,
        rows_in,
        gather_in,
        back_out,
        back_in,
        part_out,
        part_in,
        blocks,
        in_sem,
        atom_send,
        atom_recv,
        want_send,
        want_recv,
        rows_send,
        rows_recv,
        pair_send,
        pair_recv,
        back_send,
        back_recv,
        part_send,
        part_recv,
    ) = refs[2 * n_in + 4 :]
    depth = count // plane
    half = depth // 2
    own = half // 2
    per_peer = fetch.shape[0]
    local, atom_width = atoms.shape
    share = half * per_peer
    total = plane * share
    edges, width = messages.shape
    trip_count = trips.shape[1]
    tri = down_w.shape[1]
    tile = 256

    me = lax.axis_index("graph")
    my_z, my_q = me // plane, me % plane

    def far_first(step, size):
        return size // 2 + (step // 2) * (2 * (step % 2) - 1)

    def z_peer(step):
        return (my_z + far_first(step, depth)) % depth

    def q_peer(step):
        return (my_q + far_first(step, plane)) % plane

    def to_slot(step):
        return (own + far_first(step, depth)) % depth

    def from_slot(step):
        return (own - far_first(step, depth) + depth) % depth

    def at(z, q):
        return {"graph": z * plane + q}

    def remote(src, dst, send, recv, where):
        return pltpu.make_async_remote_copy(
            src_ref=src, dst_ref=dst, send_sem=send, recv_sem=recv, device_id=where, device_id_type=MESH
        )

    barrier = pltpu.get_barrier_semaphore()

    @pl.loop(1, depth)
    def _(step):
        pl.semaphore_signal(barrier, inc=1, device_id=at(z_peer(step), my_q), device_id_type=MESH)

    @pl.loop(1, plane)
    def _(step):
        pl.semaphore_signal(barrier, inc=1, device_id=at(my_z, q_peer(step)), device_id_type=MESH)

    loads = [pltpu.make_async_copy(hbm[i], vm[i], in_sem.at[i]) for i in range(n_in)]
    loads.append(pltpu.make_async_copy(blocks_hbm, blocks, in_sem.at[n_in]))
    for load in [loads[n_in]] + loads[:n_in]:
        load.start()

    loads[1].wait()
    flat = jnp.concatenate([fetch[c : c + 1, :] for c in range(per_peer)], axis=1)
    flat = jnp.broadcast_to(flat.astype(F32), (8, per_peer * count)).astype(BF16)
    from_peer = iota((per_peer * count, 128), 0)
    to_lane = iota((per_peer * count, 128), 1)
    lane_z = (my_z + (to_lane // share) * half + to_lane % half + depth - own) % depth
    lane_c = (to_lane % share) // half
    same_c = from_peer // count == lane_c
    offset = from_peer % count - lane_z * plane
    lane = iota((8, 128), 1)
    for q in range(plane):
        pick = hot(same_c & (offset == q))
        ids = dot(flat, pick).astype(jnp.int32) + (lane % half) * local
        want_out[q] = jnp.where(lane < 2 * share, ids, -1)[0:1, :]

    loads[2].wait()
    slot = slots_in[...]
    owner = slot // per_peer
    place = (owner // plane - my_z + own + depth) % depth
    slot = (place // half) * total + (owner % plane) * share + (slot % per_peer) * half + place % half
    for role in range(2):
        row = slot[role : role + 1, :]
        edge_rows[role] = hot_rows(row, 2 * total)
        slot_cols[:, role * edges : (role + 1) * edges] = hot(iota((2 * total, edges), 0) == row)

    loads[n_in].wait()
    loads[3].wait()
    live = blocks[...] * TBLK
    chunk = 512

    @pl.loop(0, trip_count // chunk)
    def _(i):
        span = pl.ds(pl.multiple_of(i * chunk, chunk), chunk)
        edge = iota((edges, chunk), 0)
        at_trip = iota((1, chunk), 1) + i * chunk
        targets = jnp.where(at_trip < live, trips[0:1, span], -1)
        tt[:, span] = hot(edge == targets)
        st[:, span] = hot(edge == trips[1:2, span])

    loads[0].wait()
    table[own] = atoms[...]

    pl.semaphore_wait(barrier, depth + plane - 2)

    def atom_copy(step, slot_at):
        return remote(atoms, table.at[slot_at], atom_send.at[step], atom_recv.at[slot_at], at(z_peer(step), my_q))

    @pl.loop(1, depth)
    def _(step):
        atom_copy(step, from_slot(step)).start()

    def want_copy(step, slot_at):
        return remote(
            want_out.at[q_peer(step)], want_in.at[slot_at], want_send.at[step], want_recv.at[slot_at], at(my_z, q_peer(step))
        )

    @pl.loop(1, plane)
    def _(step):
        want_copy(step, my_q).start()

    want_in[my_q] = want_out[my_q]

    loads[4].wait()
    rev_cols[...] = hot(iota((edges, edges), 0) == reverse[...])

    @pl.loop(0, trip_count // chunk)
    def _(i):
        span = pl.ds(pl.multiple_of(i * chunk, chunk), chunk)
        rt[:, span] = dot(rev_cols[...], tt[:, span]).astype(BF16)

    loads[5].wait()
    loads[6].wait()
    bt[...] = dot(jnp.transpose(angle_w[...].astype(F32)).astype(BF16), angular[...])
    loads[7].wait()
    loads[8].wait()
    gate[...] = dot(jnp.transpose(radial[...].astype(F32)).astype(BF16), radial_w[...])

    @pl.loop(1, plane)
    def _(step):
        want_copy(step, q_peer(step)).wait_recv()

    for q in range(plane):
        picks = hot_rows(want_in[q], half * local)
        for part in range(2):
            sel[part, q * share : (q + 1) * share, :] = picks[part * share : (part + 1) * share]

    def rows_copy(part, step, slot_at):
        return remote(
            rows_out.at[part, q_peer(step)],
            rows_in.at[part, slot_at],
            rows_send.at[part, step],
            rows_recv.at[part, slot_at],
            at(my_z, q_peer(step)),
        )

    def send_rows(part):
        column_rows = table[part * half : (part + 1) * half].reshape(half * local, atom_width)
        rows = dot(sel[part], column_rows).astype(BF16)
        rows_out[part] = rows.reshape(plane, share, atom_width)

        @pl.loop(1, plane)
        def _(step):
            rows_copy(part, step, my_q).start()

        rows_in[part, my_q] = rows_out[part, my_q]

    def wait_atoms(slot_at):
        remote(atoms, table.at[slot_at], atom_send.at[0], atom_recv.at[slot_at], at(z_peer(1), my_q)).wait_recv()

    @pl.loop(1, half)
    def _(step):
        wait_atoms((own + step) % half)

    send_rows(0)

    for part in range(2):
        sel_t[part] = jnp.transpose(sel[part].astype(F32)).astype(BF16)
    loads[9].wait()
    down_t[...] = jnp.transpose(down_w[...].astype(F32)).astype(BF16)
    loads[11].wait()
    loads[12].wait()

    @pl.loop(0, width // tile)
    def _(i):
        span = pl.ds(pl.multiple_of(i * tile, tile), tile)
        pre[:, span] = dot(messages[...], message_w[:, span])

    @pl.loop(half, depth)
    def _(slot_at):
        wait_atoms(slot_at)

    send_rows(1)

    loads[10].wait()
    loads[14].wait()
    same = dot_nt(up_ca[...], up_ca[...]) + dot_nt(up_ac[...], up_ac[...])
    cross = dot_nt(up_ac[...], up_ca[...])
    cross = cross + jnp.transpose(cross)
    for part, value in enumerate((same, cross)):
        high = value.astype(BF16)
        mix[part, :tri, :] = high
        mix[part, tri:, :] = (value - high.astype(F32)).astype(BF16)
    loads[13].wait()
    loads[15].wait()

    end_rows = [None, None]
    for part in range(2):

        @pl.loop(1, plane)
        def _(step):
            rows_copy(part, step, q_peer(step)).wait_recv()

        slot_rows = rows_in[part].reshape(total, atom_width)
        for role in range(2):
            found = dot(edge_rows[role, :, part * total : (part + 1) * total], slot_rows)
            end_rows[role] = found if part == 0 else end_rows[role] + found
    source_rows, target_rows = end_rows[0].astype(BF16), end_rows[1].astype(BF16)
    down = jnp.zeros((tri, edges), F32)
    for start in range(0, width, tile):
        span = slice(start, start + tile)
        part = pre[:, span] + dot(source_rows, source_w[:, span]) + dot(target_rows, target_w[:, span])
        pre[:, span] = part
        hidden[:, span] = (part * jax.nn.sigmoid(part) * gate[:, span]).astype(BF16)
        down = down + dot_nt(down_t[:, span], hidden[:, span])
    reduced = (down * jax.nn.sigmoid(down)).astype(BF16)
    terms = (dot(reduced, st[...]) * bt[...]).astype(BF16)
    gathered = dot_nt(terms, tt[...]).astype(BF16)
    gather_out[...] = gathered

    pair_copy = remote(gather_out, gather_in, pair_send, pair_recv, at(my_z, my_q + 1 - 2 * (my_q % 2)))
    pair_copy.start()

    def mixed(part, value):
        both = dot(mix[part], value)
        return (both[:tri] + both[tri:]).astype(BF16)

    y[...] = dot(mixed(0, gathered), tt[...])
    sigma = jax.nn.sigmoid(down)
    down_slope = sigma * (1.0 + down * (1.0 - sigma))
    for start in range(0, width, tile):
        span = slice(start, start + tile)
        part = pre[:, span]
        sigma = jax.nn.sigmoid(part)
        gate[:, span] = gate[:, span] * (sigma * (1.0 + part * (1.0 - sigma)))

    pair_copy.wait_recv()

    terms = ((y[...] + dot(mixed(1, gather_in[...]), rt[...])) * bt[...]).astype(BF16)
    down_grad = dot_nt(terms, st[...]) * down_slope
    down_grad = jnp.transpose(down_grad).astype(BF16)
    ends = [jnp.zeros((edges, atom_width), F32) for _ in range(2)]
    for start in range(0, width, tile):
        span = slice(start, start + tile)
        part = (dot(down_grad, down_t[:, span]) * gate[:, span]).astype(BF16)
        grad[:, span] = part
        ends[0] = ends[0] + dot_nt(part, source_w[:, span])
        ends[1] = ends[1] + dot_nt(part, target_w[:, span])
    ends = jnp.concatenate([ends[0].astype(BF16), ends[1].astype(BF16)], axis=0)

    def back_copy(part, step, slot_at):
        return remote(
            back_out.at[part, q_peer(step)],
            back_in.at[part, slot_at],
            back_send.at[part, step],
            back_recv.at[part, slot_at],
            at(my_z, q_peer(step)),
        )

    for part in (1, 0):
        back = dot(slot_cols[part * total : (part + 1) * total, :], ends).astype(BF16)
        back_out[part] = back.reshape(plane, share, atom_width)

        @pl.loop(1, plane)
        def _(step):
            back_copy(part, step, my_q).start()

        back_in[part, my_q] = back_out[part, my_q]

    mine = jnp.transpose(gather_out[...].astype(F32)).astype(BF16)
    theirs = jnp.transpose(dot(gather_in[...], rev_cols[...])).astype(BF16)
    for start in range(0, width, tile):
        span = slice(start, start + tile)
        raised = dot(mine, up_ca[:, span]) + dot(theirs, up_ac[:, span])
        updated_out[:, span] = raised.astype(BF16)

    def part_copy(step, slot_at):
        return remote(
            part_out.at[to_slot(step)], part_in.at[slot_at], part_send.at[step], part_recv.at[slot_at], at(z_peer(step), my_q)
        )

    for part in (1, 0):

        @pl.loop(1, plane)
        def _(step):
            back_copy(part, step, q_peer(step)).wait_recv()

        sums = dot(sel_t[part], back_in[part].reshape(total, atom_width)).astype(BF16)
        part_out[part * half : (part + 1) * half] = sums.reshape(half, local, atom_width)

        @pl.loop(1 if part else half + 1, half + 1 if part else depth)
        def _(step):
            part_copy(step, from_slot(step)).start()

    part_in[own] = part_out[own]

    @pl.loop(0, width // tile)
    def _(i):
        span = pl.ds(pl.multiple_of(i * tile, tile), tile)
        message_out[:, span] = dot_nt(grad[...], message_w[span, :]).astype(BF16)

    @pl.loop(1, depth)
    def _(step):
        slot_at = (own + step) % depth
        remote(
            part_out.at[0], part_in.at[slot_at], part_send.at[0], part_recv.at[slot_at], at(z_peer(1), my_q)
        ).wait_recv()

    owned = part_in[0].astype(F32)
    for z in range(1, depth):
        owned = owned + part_in[z].astype(F32)
    atom_out[...] = owned

    @pl.loop(1, depth)
    def _(step):
        atom_copy(step, from_slot(step)).wait_send()
        part_copy(step, from_slot(step)).wait_send()

    @pl.loop(1, plane)
    def _(step):
        want_copy(step, my_q).wait_send()
        for part in range(2):
            rows_copy(part, step, my_q).wait_send()
            back_copy(part, step, my_q).wait_send()

    pair_copy.wait_send()


def shards(
    atoms,
    fetch_rows,
    edge_slots,
    messages,
    radial,
    angular,
    trip_edges,
    trip_blocks,
    reverse_slot,
    message_weight,
    source_weight,
    target_weight,
    radial_weight,
    down_weight,
    angle_weight,
    up_ca_weight,
    up_ac_weight,
):
    count = lax.axis_size("graph")
    plane = PLANE
    depth = count // plane
    local, atom_width = atoms.shape
    edges, width = messages.shape
    tri = down_weight.shape[1]
    trip_count = trip_edges.shape[1]
    per_peer = fetch_rows.shape[2]
    half = depth // 2
    share = half * per_peer
    total = plane * share
    fetch = jnp.transpose(fetch_rows[0])
    operands = (
        atoms,
        fetch,
        edge_slots,
        trip_edges,
        reverse_slot.reshape(1, edges),
        angular,
        angle_weight,
        radial,
        radial_weight,
        down_weight,
        up_ca_weight,
        messages,
        message_weight,
        source_weight,
        up_ac_weight,
        target_weight,
    )
    V = pltpu.VMEM
    DMA = pltpu.SemaphoreType.DMA
    scratch = [V(x.shape, x.dtype) for x in operands] + [
        V((edges, trip_count), BF16),
        V((edges, trip_count), BF16),
        V((tri, trip_count), F32),
        V((edges, width), F32),
        V((edges, width), F32),
        V((edges, width), BF16),
        V((edges, width), BF16),
        V((tri, width), BF16),
        V((edges, trip_count), BF16),
        V((tri, trip_count), F32),
        V((2, 2 * tri, tri), BF16),
        V((2, edges, 2 * total), BF16),
        V((2 * total, 2 * edges), BF16),
        V((edges, edges), BF16),
        V((2, total, half * local), BF16),
        V((2, half * local, total), BF16),
        V((tri, edges), BF16),
        V((depth, local, atom_width), BF16),
        V((plane, 1, 128), jnp.int32),
        V((plane, 1, 128), jnp.int32),
        V((2, plane, share, atom_width), BF16),
        V((2, plane, share, atom_width), BF16),
        V((tri, edges), BF16),
        V((2, plane, share, atom_width), BF16),
        V((2, plane, share, atom_width), BF16),
        V((depth, local, atom_width), BF16),
        V((depth, local, atom_width), BF16),
        V((1, 1), jnp.int32),
        DMA((17,)),
        DMA((depth,)),
        DMA((depth,)),
        DMA((plane,)),
        DMA((plane,)),
        DMA((2, plane)),
        DMA((2, plane)),
        DMA,
        DMA,
        DMA((2, plane)),
        DMA((2, plane)),
        DMA((depth,)),
        DMA((depth,)),
    ]
    return pl.pallas_call(
        functools.partial(kernel, plane, count),
        out_shape=(
            pltpu.VMEM((edges, width), BF16),
            pltpu.VMEM((edges, width), BF16),
            pltpu.VMEM((local, atom_width), F32),
        ),
        in_specs=[pl.BlockSpec(memory_space=pl.ANY)] * (1 + len(operands)),
        out_specs=[pl.BlockSpec(memory_space=pltpu.VMEM)] * 3,
        scratch_shapes=scratch,
        compiler_params=pltpu.CompilerParams(
            collective_id=0, has_side_effects=True, vmem_limit_bytes=VMEM
        ),
        cost_estimate=pl.CostEstimate(flops=3_000_000_000, bytes_accessed=8_000_000, transcendentals=1_000_000),
    )(trip_blocks.reshape(1, 1), *operands)


def solution(mesh):
    both = ("dp", "graph")
    rows, lanes = P(both, None), P(None, both)
    placed = (
        rows,
        P(both, None, None),
        lanes,
        rows,
        lanes,
        lanes,
        lanes,
        P(both),
        P(both),
    ) + (P(),) * 8
    return jax.shard_map(
        shards,
        mesh=mesh,
        in_specs=placed,
        out_specs=(rows, rows, rows),
        check_vma=False,
    )
```

time: 53.2 us -> 52.3 us (0.983)
  the two profiles are of different devices: /device:TPU:24 before, /device:TPU:1 now
where the time goes in v3:
time: 52.3 us; the launch traced here: 52.2 us
  Pallas kernels  48.7 us (93%)
  local copies, waits for them, and re-layouts  2.19 us (4%)
  between operations  1.29 us (2%)
    pallas_call x1, Pallas kernels, shards(): pl.pallas_call(functools.partial(kernel, plane, count), out_shape=(pltpu....  48.7 us
    unnamed x3, local copies, waits for them, and re-layouts  2.19 us

profile of v3, /device:TPU:1, one launch (start us, length us, event | category | flops | bytes accessed | tf_op | source)
XLA Modules:
  0.0 52.2 jit_solution(12353780972524871702)
XLA Ops:
  1.3 48.7 %shard_map.184 = (bf16[256,1024]{1,0:T(8,128)(2,1)S(1)}, bf16[256,1024]{1,0:T(8,128)(2,1)S(1)}, f32[16,256]{1,0:T(8,128)S(1)}) custom-call(s32[1,1]{1,0:T(1,128)} %bitcast.5.refs_0_, bf16[16,256]{1,0:T(8,128)(2,1)} %refs_1_.1, s32[4,128]{1,0:T(4,128)} %bitcast.6, s32[2,256]{1,0:T(2,128)} %refs_3_.1, s32[2,2048]{1,0:T(2,128)} %refs_4_.1, s32[1,256]{1,0:T(1,128)} %bitcast.7, ...), custom_call_target="tpu_custom_call" | custom-call | flops 3000000000 | bytes 8000000 | tf_op jit(solution)/shard_map/pallas_call | solution.py:540
  50.0 0.8 %copy.23 = bf16[256,1024]{1,0:T(8,128)(2,1)} copy(bf16[256,1024]{1,0:T(8,128)(2,1)S(1)} %get-tuple-element.3) | data formatting | bytes 1048576
  50.8 0.6 %copy.25 = f32[16,256]{1,0:T(8,128)} copy(f32[16,256]{1,0:T(8,128)S(1)} %get-tuple-element.5) | data formatting | bytes 32768
  51.4 0.8 %copy.24 = bf16[256,1024]{1,0:T(8,128)(2,1)} copy(bf16[256,1024]{1,0:T(8,128)(2,1)S(1)} %get-tuple-element.4) | data formatting | bytes 1048576

commit v4 on v3

--- a/solution.py
+++ b/solution.py
@@ -151,6 +151,12 @@
             src_ref=src, dst_ref=dst, send_sem=send, recv_sem=recv, device_id=where, device_id_type=MESH
         )
 
+    def wait_recv(group, recv):
+        remote(group, group, atom_send, recv, at(z_peer(1), my_q)).wait_recv()
+
+    def wait_send(group, send):
+        remote(group, group, send, atom_recv.at[0], at(z_peer(1), my_q)).wait_send()
+
     barrier = pltpu.get_barrier_semaphore()
 
     @pl.loop(1, depth)
@@ -211,7 +217,7 @@
     pl.semaphore_wait(barrier, depth + plane - 2)
 
     def atom_copy(step, slot_at):
-        return remote(atoms, table.at[slot_at], atom_send.at[step], atom_recv.at[slot_at], at(z_peer(step), my_q))
+        return remote(atoms, table.at[slot_at], atom_send, atom_recv.at[slot_at // half], at(z_peer(step), my_q))
 
     @pl.loop(1, depth)
     def _(step):
@@ -219,7 +225,7 @@
 
     def want_copy(step, slot_at):
         return remote(
-            want_out.at[q_peer(step)], want_in.at[slot_at], want_send.at[step], want_recv.at[slot_at], at(my_z, q_peer(step))
+            want_out.at[q_peer(step)], want_in.at[slot_at], want_send, want_recv, at(my_z, q_peer(step))
         )
 
     @pl.loop(1, plane)
@@ -243,9 +249,7 @@
     loads[8].wait()
     gate[...] = dot(jnp.transpose(radial[...].astype(F32)).astype(BF16), radial_w[...])
 
-    @pl.loop(1, plane)
-    def _(step):
-        want_copy(step, q_peer(step)).wait_recv()
+    wait_recv(want_in.at[pl.ds(0, plane - 1)], want_recv)
 
     for q in range(plane):
         picks = hot_rows(want_in[q], half * local)
@@ -256,8 +260,8 @@
         return remote(
             rows_out.at[part, q_peer(step)],
             rows_in.at[part, slot_at],
-            rows_send.at[part, step],
-            rows_recv.at[part, slot_at],
+            rows_send.at[part],
+            rows_recv.at[part],
             at(my_z, q_peer(step)),
         )
 
@@ -272,13 +276,7 @@
 
         rows_in[part, my_q] = rows_out[part, my_q]
 
-    def wait_atoms(slot_at):
-        remote(atoms, table.at[slot_at], atom_send.at[0], atom_recv.at[slot_at], at(z_peer(1), my_q)).wait_recv()
-
-    @pl.loop(1, half)
-    def _(step):
-        wait_atoms((own + step) % half)
-
+    wait_recv(table.at[pl.ds(0, half - 1)], atom_recv.at[0])
     send_rows(0)
 
     for part in range(2):
@@ -293,9 +291,7 @@
         span = pl.ds(pl.multiple_of(i * tile, tile), tile)
         pre[:, span] = dot(messages[...], message_w[:, span])
 
-    @pl.loop(half, depth)
-    def _(slot_at):
-        wait_atoms(slot_at)
+    wait_recv(table.at[pl.ds(half, half)], atom_recv.at[1])
 
     send_rows(1)
 
@@ -313,11 +309,7 @@
 
     end_rows = [None, None]
     for part in range(2):
-
-        @pl.loop(1, plane)
-        def _(step):
-            rows_copy(part, step, q_peer(step)).wait_recv()
-
+        wait_recv(rows_in.at[part, pl.ds(0, plane - 1)], rows_recv.at[part])
         slot_rows = rows_in[part].reshape(total, atom_width)
         for role in range(2):
             found = dot(edge_rows[role, :, part * total : (part + 1) * total], slot_rows)
@@ -369,8 +361,8 @@
         return remote(
             back_out.at[part, q_peer(step)],
             back_in.at[part, slot_at],
-            back_send.at[part, step],
-            back_recv.at[part, slot_at],
+            back_send.at[part],
+            back_recv.at[part],
             at(my_z, q_peer(step)),
         )
 
@@ -393,15 +385,11 @@
 
     def part_copy(step, slot_at):
         return remote(
-            part_out.at[to_slot(step)], part_in.at[slot_at], part_send.at[step], part_recv.at[slot_at], at(z_peer(step), my_q)
+            part_out.at[to_slot(step)], part_in.at[slot_at], part_send, part_recv, at(z_peer(step), my_q)
         )
 
     for part in (1, 0):
-
-        @pl.loop(1, plane)
-        def _(step):
-            back_copy(part, step, q_peer(step)).wait_recv()
-
+        wait_recv(back_in.at[part, pl.ds(0, plane - 1)], back_recv.at[part])
         sums = dot(sel_t[part], back_in[part].reshape(total, atom_width)).astype(BF16)
         part_out[part * half : (part + 1) * half] = sums.reshape(half, local, atom_width)
 
@@ -416,30 +404,19 @@
         span = pl.ds(pl.multiple_of(i * tile, tile), tile)
         message_out[:, span] = dot_nt(grad[...], message_w[span, :]).astype(BF16)
 
-    @pl.loop(1, depth)
-    def _(step):
-        slot_at = (own + step) % depth
-        remote(
-            part_out.at[0], part_in.at[slot_at], part_send.at[0], part_recv.at[slot_at], at(z_peer(1), my_q)
-        ).wait_recv()
+    wait_recv(part_in.at[pl.ds(0, depth - 1)], part_recv)
 
     owned = part_in[0].astype(F32)
     for z in range(1, depth):
         owned = owned + part_in[z].astype(F32)
     atom_out[...] = owned
 
-    @pl.loop(1, depth)
-    def _(step):
-        atom_copy(step, from_slot(step)).wait_send()
-        part_copy(step, from_slot(step)).wait_send()
-
-    @pl.loop(1, plane)
-    def _(step):
-        want_copy(step, my_q).wait_send()
-        for part in range(2):
-            rows_copy(part, step, my_q).wait_send()
-            back_copy(part, step, my_q).wait_send()
-
+    wait_send(table.at[pl.ds(0, depth - 1)], atom_send)
+    wait_send(want_out.at[pl.ds(0, plane - 1)], want_send)
+    for part in range(2):
+        wait_send(rows_out.at[part, pl.ds(0, plane - 1)], rows_send.at[part])
+        wait_send(back_out.at[part, pl.ds(0, plane - 1)], back_send.at[part])
+    wait_send(part_out.at[pl.ds(0, depth - 1)], part_send)
     pair_copy.wait_send()
 
 
@@ -524,18 +501,18 @@
         V((depth, local, atom_width), BF16),
         V((1, 1), jnp.int32),
         DMA((17,)),
-        DMA((depth,)),
-        DMA((depth,)),
-        DMA((plane,)),
-        DMA((plane,)),
-        DMA((2, plane)),
-        DMA((2, plane)),
-        DMA,
-        DMA,
-        DMA((2, plane)),
-        DMA((2, plane)),
-        DMA((depth,)),
-        DMA((depth,)),
+        DMA,
+        DMA((2,)),
+        DMA,
+        DMA,
+        DMA((2,)),
+        DMA((2,)),
+        DMA,
+        DMA,
+        DMA((2,)),
+        DMA((2,)),
+        DMA,
+        DMA,
     ]
     return pl.pallas_call(
         functools.partial(kernel, plane, count),

time: 52.3 us -> 50.9 us (0.973)
  Pallas kernels: 48.7 us -> 47.3 us
    pallas_call x1, Pallas kernels: 48.7 us -> 47.3 us  [shards(): pl.pallas_call(functools.partial(kernel, plane, count), out_shape=(pltpu....]
where the time goes in v4:
time: 50.9 us; the launch traced here: 50.8 us
  Pallas kernels  47.3 us (93%)
  local copies, waits for them, and re-layouts  2.19 us (4%)
  between operations  1.29 us (3%)
    pallas_call x1, Pallas kernels, shards(): pl.pallas_call(functools.partial(kernel, plane, count), out_shape=(pltpu....  47.3 us
    unnamed x3, local copies, waits for them, and re-layouts  2.19 us

profile of v4, /device:TPU:1, one launch (start us, length us, event | category | flops | bytes accessed | tf_op | source)
XLA Modules:
  0.0 50.8 jit_solution(12813086965181601685)
XLA Ops:
  1.3 47.3 %shard_map.184 = (bf16[256,1024]{1,0:T(8,128)(2,1)S(1)}, bf16[256,1024]{1,0:T(8,128)(2,1)S(1)}, f32[16,256]{1,0:T(8,128)S(1)}) custom-call(s32[1,1]{1,0:T(1,128)} %bitcast.5.refs_0_, bf16[16,256]{1,0:T(8,128)(2,1)} %refs_1_.1, s32[4,128]{1,0:T(4,128)} %bitcast.6, s32[2,256]{1,0:T(2,128)} %refs_3_.1, s32[2,2048]{1,0:T(2,128)} %refs_4_.1, s32[1,256]{1,0:T(1,128)} %bitcast.7, ...), custom_call_target="tpu_custom_call" | custom-call | flops 3000000000 | bytes 8000000 | tf_op jit(solution)/shard_map/pallas_call | solution.py:517
  48.6 0.8 %copy.23 = bf16[256,1024]{1,0:T(8,128)(2,1)} copy(bf16[256,1024]{1,0:T(8,128)(2,1)S(1)} %get-tuple-element.3) | data formatting | bytes 1048576
  49.4 0.6 %copy.25 = f32[16,256]{1,0:T(8,128)} copy(f32[16,256]{1,0:T(8,128)S(1)} %get-tuple-element.5) | data formatting | bytes 32768
  50.0 0.8 %copy.24 = bf16[256,1024]{1,0:T(8,128)(2,1)} copy(bf16[256,1024]{1,0:T(8,128)(2,1)S(1)} %get-tuple-element.4) | data formatting | bytes 1048576

commit v5 on v4

--- a/solution.py
+++ b/solution.py
@@ -50,8 +50,8 @@
 ):
     n_in = 16
     blocks_hbm, *hbm = refs[: n_in + 1]
-    updated_out, message_out, atom_out = refs[n_in + 1 : n_in + 4]
-    vm = refs[n_in + 4 : 2 * n_in + 4]
+    edge_out, atom_out = refs[n_in + 1 : n_in + 3]
+    vm = refs[n_in + 3 : 2 * n_in + 3]
     (
         atoms,
         fetch,
@@ -79,6 +79,8 @@
         hidden,
         grad,
         down_t,
+        tn,
+        sn,
         rt,
         y,
         mix,
@@ -112,7 +114,7 @@
         back_recv,
         part_send,
         part_recv,
-    ) = refs[2 * n_in + 4 :]
+    ) = refs[2 * n_in + 3 :]
     depth = count // plane
     half = depth // 2
     own = half // 2
@@ -233,6 +235,13 @@
         want_copy(step, my_q).start()
 
     want_in[my_q] = want_out[my_q]
+
+    @pl.loop(0, trip_count // chunk)
+    def _(i):
+        span = pl.ds(pl.multiple_of(i * chunk, chunk), chunk)
+        at_trip = iota((1, chunk), 1) + i * chunk
+        tn[span, :] = hot_rows(jnp.where(at_trip < live, trips[0:1, span], -1), edges)
+        sn[span, :] = hot_rows(trips[1:2, span], edges)
 
     loads[4].wait()
     rev_cols[...] = hot(iota((edges, edges), 0) == reverse[...])
@@ -324,7 +333,7 @@
         down = down + dot_nt(down_t[:, span], hidden[:, span])
     reduced = (down * jax.nn.sigmoid(down)).astype(BF16)
     terms = (dot(reduced, st[...]) * bt[...]).astype(BF16)
-    gathered = dot_nt(terms, tt[...]).astype(BF16)
+    gathered = dot(terms, tn[...]).astype(BF16)
     gather_out[...] = gathered
 
     pair_copy = remote(gather_out, gather_in, pair_send, pair_recv, at(my_z, my_q + 1 - 2 * (my_q % 2)))
@@ -346,7 +355,7 @@
     pair_copy.wait_recv()
 
     terms = ((y[...] + dot(mixed(1, gather_in[...]), rt[...])) * bt[...]).astype(BF16)
-    down_grad = dot_nt(terms, st[...]) * down_slope
+    down_grad = dot(terms, sn[...]) * down_slope
     down_grad = jnp.transpose(down_grad).astype(BF16)
     ends = [jnp.zeros((edges, atom_width), F32) for _ in range(2)]
     for start in range(0, width, tile):
@@ -381,7 +390,7 @@
     for start in range(0, width, tile):
         span = slice(start, start + tile)
         raised = dot(mine, up_ca[:, span]) + dot(theirs, up_ac[:, span])
-        updated_out[:, span] = raised.astype(BF16)
+        edge_out[:edges, span] = raised.astype(BF16)
 
     def part_copy(step, slot_at):
         return remote(
@@ -402,7 +411,7 @@
     @pl.loop(0, width // tile)
     def _(i):
         span = pl.ds(pl.multiple_of(i * tile, tile), tile)
-        message_out[:, span] = dot_nt(grad[...], message_w[span, :]).astype(BF16)
+        edge_out[edges:, span] = dot_nt(grad[...], message_w[span, :]).astype(BF16)
 
     wait_recv(part_in.at[pl.ds(0, depth - 1)], part_recv)
 
@@ -480,6 +489,8 @@
         V((edges, width), BF16),
         V((edges, width), BF16),
         V((tri, width), BF16),
+        V((trip_count, edges), BF16),
+        V((trip_count, edges), BF16),
         V((edges, trip_count), BF16),
         V((tri, trip_count), F32),
         V((2, 2 * tri, tri), BF16),
@@ -514,21 +525,21 @@
         DMA,
         DMA,
     ]
-    return pl.pallas_call(
+    both, atom_grad = pl.pallas_call(
         functools.partial(kernel, plane, count),
         out_shape=(
-            pltpu.VMEM((edges, width), BF16),
-            pltpu.VMEM((edges, width), BF16),
+            pltpu.VMEM((2 * edges, width), BF16),
             pltpu.VMEM((local, atom_width), F32),
         ),
         in_specs=[pl.BlockSpec(memory_space=pl.ANY)] * (1 + len(operands)),
-        out_specs=[pl.BlockSpec(memory_space=pltpu.VMEM)] * 3,
+        out_specs=[pl.BlockSpec(memory_space=pltpu.VMEM)] * 2,
         scratch_shapes=scratch,
         compiler_params=pltpu.CompilerParams(
             collective_id=0, has_side_effects=True, vmem_limit_bytes=VMEM
         ),
         cost_estimate=pl.CostEstimate(flops=3_000_000_000, bytes_accessed=8_000_000, transcendentals=1_000_000),
     )(trip_blocks.reshape(1, 1), *operands)
+    return both[:edges], both[edges:], atom_grad
 
 
 def solution(mesh):

time: 50.9 us -> 49.9 us (0.980)
  local copies, waits for them, and re-layouts: 2.19 us -> 1.64 us
    unnamed x3 -> x1, local copies, waits for them, and re-layouts: 2.19 us -> 0.6 us
    slice x0 -> x1, local copies, waits for them, and re-layouts: none -> 1.03 us  [shards(): return (both[:edges], both[edges:], atom_grad)]
where the time goes in v5:
time: 49.9 us; the launch traced here: 49.8 us
  Pallas kernels  46.9 us (94%)
  local copies, waits for them, and re-layouts  1.64 us (3%)
  between operations  1.29 us (3%)
    pallas_call x1, Pallas kernels, shards(): pl.pallas_call(functools.partial(kernel, plane, count), out_shape=(pltpu....  46.9 us
    slice x1, local copies, waits for them, and re-layouts, shards(): return (both[:edges], both[edges:], atom_grad)  1.03 us

profile of v5, /device:TPU:1, one launch (start us, length us, event | category | flops | bytes accessed | tf_op | source)
XLA Modules:
  0.0 49.8 jit_solution(9391968546249449739)
XLA Ops:
  1.3 46.9 %shard_map.184 = (bf16[512,1024]{1,0:T(8,128)(2,1)S(1)}, f32[16,256]{1,0:T(8,128)S(1)}) custom-call(s32[1,1]{1,0:T(1,128)} %bitcast.5.refs_0_, bf16[16,256]{1,0:T(8,128)(2,1)} %refs_1_.1, s32[4,128]{1,0:T(4,128)} %bitcast.6, s32[2,256]{1,0:T(2,128)} %refs_3_.1, s32[2,2048]{1,0:T(2,128)} %refs_4_.1, s32[1,256]{1,0:T(1,128)} %bitcast.7, ...), custom_call_target="tpu_custom_call" | custom-call | flops 3000000000 | bytes 8000000 | tf_op jit(solution)/shard_map/pallas_call | solution.py:528
  48.2 1.0 %fusion = (bf16[256,1024]{1,0:T(8,128)(2,1)}, bf16[256,1024]{1,0:T(8,128)(2,1)}) fusion(bf16[512,1024]{1,0:T(8,128)(2,1)S(1)} %get-tuple-element.5), kind=kLoop, calls=%fused_computation | loop fusion | bytes 2097152 | tf_op jit(solution)/shard_map/slice | solution.py:542
  49.2 0.6 %copy.21 = f32[16,256]{1,0:T(8,128)} copy(f32[16,256]{1,0:T(8,128)S(1)} %get-tuple-element.11) | data formatting | bytes 32768

commit v6 on v5

--- a/solution.py
+++ b/solution.py
@@ -125,7 +125,7 @@
     edges, width = messages.shape
     trip_count = trips.shape[1]
     tri = down_w.shape[1]
-    tile = 256
+    tile = 512
 
     me = lax.axis_index("graph")
     my_z, my_q = me // plane, me % plane
@@ -254,10 +254,6 @@
     loads[5].wait()
     loads[6].wait()
     bt[...] = dot(jnp.transpose(angle_w[...].astype(F32)).astype(BF16), angular[...])
-    loads[7].wait()
-    loads[8].wait()
-    gate[...] = dot(jnp.transpose(radial[...].astype(F32)).astype(BF16), radial_w[...])
-
     wait_recv(want_in.at[pl.ds(0, plane - 1)], want_recv)
 
     for q in range(plane):
@@ -288,6 +284,10 @@
     wait_recv(table.at[pl.ds(0, half - 1)], atom_recv.at[0])
     send_rows(0)
 
+    wait_recv(table.at[pl.ds(half, half)], atom_recv.at[1])
+
+    send_rows(1)
+
     for part in range(2):
         sel_t[part] = jnp.transpose(sel[part].astype(F32)).astype(BF16)
     loads[9].wait()
@@ -300,9 +300,9 @@
         span = pl.ds(pl.multiple_of(i * tile, tile), tile)
         pre[:, span] = dot(messages[...], message_w[:, span])
 
-    wait_recv(table.at[pl.ds(half, half)], atom_recv.at[1])
-
-    send_rows(1)
+    loads[7].wait()
+    loads[8].wait()
+    gate[...] = dot(jnp.transpose(radial[...].astype(F32)).astype(BF16), radial_w[...])
 
     loads[10].wait()
     loads[14].wait()

time: 49.9 us -> 48.5 us (0.972); the launches traced: 49.8 us -> 47.8 us
  Pallas kernels: 46.9 us -> 44.8 us
    pallas_call x1, Pallas kernels: 46.9 us -> 44.8 us  [shards(): pl.pallas_call(functools.partial(kernel, plane, count), out_shape=(pltpu....]
where the time goes in v6:
time: 48.5 us; the launch traced here: 47.8 us
  Pallas kernels  44.8 us (92%)
  local copies, waits for them, and re-layouts  1.64 us (3%)
  between operations  1.29 us (3%)
    pallas_call x1, Pallas kernels, shards(): pl.pallas_call(functools.partial(kernel, plane, count), out_shape=(pltpu....  44.8 us
    slice x1, local copies, waits for them, and re-layouts, shards(): return (both[:edges], both[edges:], atom_grad)  1.03 us

profile of v6, /device:TPU:1, one launch (start us, length us, event | category | flops | bytes accessed | tf_op | source)
XLA Modules:
  0.0 47.8 jit_solution(5479881589950547907)
XLA Ops:
  1.3 44.8 %shard_map.184 = (bf16[512,1024]{1,0:T(8,128)(2,1)S(1)}, f32[16,256]{1,0:T(8,128)S(1)}) custom-call(s32[1,1]{1,0:T(1,128)} %bitcast.5.refs_0_, bf16[16,256]{1,0:T(8,128)(2,1)} %refs_1_.1, s32[4,128]{1,0:T(4,128)} %bitcast.6, s32[2,256]{1,0:T(2,128)} %refs_3_.1, s32[2,2048]{1,0:T(2,128)} %refs_4_.1, s32[1,256]{1,0:T(1,128)} %bitcast.7, ...), custom_call_target="tpu_custom_call" | custom-call | flops 3000000000 | bytes 8000000 | tf_op jit(solution)/shard_map/pallas_call | solution.py:528
  46.1 1.0 %fusion = (bf16[256,1024]{1,0:T(8,128)(2,1)}, bf16[256,1024]{1,0:T(8,128)(2,1)}) fusion(bf16[512,1024]{1,0:T(8,128)(2,1)S(1)} %get-tuple-element.5), kind=kLoop, calls=%fused_computation | loop fusion | bytes 2097152 | tf_op jit(solution)/shard_map/slice | solution.py:542
  47.2 0.6 %copy.21 = f32[16,256]{1,0:T(8,128)} copy(f32[16,256]{1,0:T(8,128)S(1)} %get-tuple-element.11) | data formatting | bytes 32768
